TPU v7x, 512 devices: a whole 4x8x8 slice. The times are simulated.
512 devices in a mesh: dp: 64 (over y, z_lo, x), mp: 8 (over z_hi, core).
Axes of the slice: x: 4, y: 8, z: 8 (z_hi: 4, z_lo: 2; z = z_hi * 2 + z_lo), core: 2. Of those that a mesh axis runs over, the one named last changes fastest.
Arguments:
- grad_partials: bfloat16 [64, 64, 73728], P('dp', None, 'mp'), may hold values from -240 to 240
- master: float32 [64, 73728], P('dp', 'mp'), may hold values from -6 to 6
- row_state: float32 [64], P('dp'), may hold values from 10 to 10000
- col_state: float32 [73728], P('mp'), may hold values from 10 to 10000
Outputs:
- master_new: float32 [64, 73728], P('dp', 'mp')
- weight_full: bfloat16 [64, 73728], P(None, 'mp')
- row_new: float32 [64], P('dp')
- col_new: float32 [73728], P('mp')
All inputs are finite; a program needn't handle non-finite values.
Results may differ from a plain program's by a relative error of at most 0.0013.
Values may be sent and summed in bfloat16 or wider, within the bound.
A program may use at most 64 MiB of HBM per device.

v0:
```python
import jax
import jax.numpy as jnp
from jax import lax
from jax.sharding import PartitionSpec as P

FF = 73728


decay_rate = 0.5
clip_level = 1.0
step_size = 0.5
tiny_term = 1e-30


def per_device(grad_partials, master, row_state, col_state):
    local_part = grad_partials[0]
    total_rows = local_part.shape[0]
    gradient = lax.psum_scatter(
        local_part.astype(jnp.float32), "dp", scatter_dimension=0, tiled=True
    )
    square = gradient * gradient
    row_total = lax.psum(jnp.sum(square, axis=1), "mp")
    row_new = decay_rate * row_state + (1.0 - decay_rate) * (row_total / FF + tiny_term)
    col_part = jnp.sum(square, axis=0)
    col_total, row_sum = lax.psum((col_part, jnp.sum(row_new)), "dp")
    col_new = decay_rate * col_state + (1.0 - decay_rate) * (col_total / total_rows + tiny_term)
    mean_row = row_sum / total_rows
    update = gradient * lax.rsqrt(row_new[:, None] * col_new[None, :] / mean_row)
    energy = lax.psum(jnp.sum(update * update), ("dp", "mp"))
    scale = jnp.maximum(1.0, jnp.sqrt(energy / (total_rows * FF)) / clip_level)
    master_new = master - step_size * (update / scale)
    weight_full = lax.all_gather(master_new.astype(jnp.bfloat16), "dp", axis=0, tiled=True)
    return (master_new, weight_full, row_new, col_new)


def solution(mesh):
    in_specs = (P("dp", None, "mp"), P("dp", "mp"), P("dp"), P("mp"))
    out_specs = (P("dp", "mp"), P(None, "mp"), P("dp"), P("mp"))
    return jax.shard_map(
        per_device, mesh=mesh, in_specs=in_specs, out_specs=out_specs, check_vma=False
    )
```

profile of v0, /device:TPU:6, one launch (start us, length us, event | category | flops | bytes accessed | tf_op | source)
XLA Modules:
  0.0 1356.9 jit_solution(17929799693738341903)
XLA Ops:
  7.2 0.0 copy-start
  7.2 0.0 copy-start.1
  7.2 0.0 all-reduce.4.cloned.1.call-start
  7.2 2.8 bitcast_convert_fusion
  10.0 0.0 all-reduce.4.cloned.1.call-update
  10.1 0.0 all-gather.3.cloned.1.call-start
  10.8 1.2 dynamic-slice
  12.0 611.9 %all-reduce.4.cloned.1.call-done = f32[64,9216]{1,0:T(8,128)} async-done(((f32[64,9216]{1,0:T(8,128)}), f32[64,9216]{1,0:T(8,128)}) %all-reduce.4.cloned.1.call-update) | async-done | bytes 2359312
  624.0 2.2 fusion
  626.1 14.8 %psum.29 = f32[1]{0:T(128)} all-reduce(f32[1]{0:T(128)} %bitcast.3), channel_id=1, replica_groups=mesh['dp'=64,'mp'=8] {'mp'}, use_global_device_ids=true, to_apply=%region_3.0 | all-reduce | flops 1 | bytes 8 | tf_op jit(solution)/shard_map/psum | solution.py:22
  641.6 297.0 %all-reduce.1 = (f32[]{:T(128)}, f32[9216]{0:T(1024)S(1)}) all-reduce(f32[]{:T(128)} %bitcast.4, f32[9216]{0:T(1024)S(1)} %bitcast.16), channel_id=1, replica_groups=mesh['dp'=64,'mp'=8] {'dp'}, use_global_device_ids=true, to_apply=%region_4.0 | all-reduce | flops 9217 | bytes 73736 | tf_op jit(solution)/shard_map/psum | solution.py:25
  939.3 0.0 copy-done
  939.4 0.6 broadcast_multiply_fusion
  940.0 2.2 multiply_reduce_fusion
  942.2 103.7 %psum.31 = f32[]{:T(128)} all-reduce(f32[]{:T(128)} %multiply_reduce_fusion), channel_id=1, replica_groups=mesh['dp'=64,'mp'=8] {'dp','mp'}, use_global_device_ids=true, to_apply=%region_6.0 | all-reduce | flops 1 | bytes 8 | tf_op jit(solution)/shard_map/psum | solution.py:29
  1046.6 0.0 copy-done.1
  1046.6 2.2 convert_bitcast_fusion
  1048.8 0.0 all-gather.3.cloned.1.call-update
  1048.8 297.1 %all-gather.3.cloned.1.call-done = bf16[64,1,9216]{2,1,0:T(2,128)(2,1)} async-done(((bf16[1,1,9216]{2,1,0:T(2,128)(2,1)}), bf16[64,1,9216]{2,1,0:T(2,128)(2,1)}) %all-gather.3.cloned.1.call-update) | async-done | bytes 1179664 | tf_op jit(solution)/shard_map/all_gather | solution.py:32
  1345.9 3.1 copy.10
Async XLA Ops:
  7.2 932.2 %copy-start = (f32[9216]{0:T(1024)S(1)}, f32[9216]{0:T(1024)}, u32[]{:S(2)}) copy-start(f32[9216]{0:T(1024)} %param.7) | copy-start | bytes 110596
  7.2 1039.4 %copy-start.1 = (f32[1,9216]{1,0:T(1,128)S(1)}, f32[1,9216]{1,0:T(1,128)}, u32[]{:S(2)}) copy-start(f32[1,9216]{1,0:T(1,128)} %param.5) | copy-start | bytes 110596
  7.2 616.8 %all-reduce.4.cloned.1.call-start = ((), (), s32[]{:S(2)}) async-start(), calls=%async_computation.1 | async-start | bytes 4718592
  10.1 1335.8 %all-gather.3.cloned.1.call-start = ((), (), s32[]{:S(2)}) async-start(), calls=%async_computation | async-start | bytes 2396160 | tf_op jit(solution)/shard_map/all_gather | solution.py:32
Sparse Core Ops, SparseCore 0:
  10.9 612.9 all-reduce.3
  1048.9 296.9 all-gather.2
where the time goes:
time: 1360 us
  waiting for transfers between devices  909 us (67%)
  blocking collectives  416 us (31%)
  between operations  17.9 us (1%)
    unnamed x3, waiting for transfers between devices  612 us
    all_gather x1, waiting for transfers between devices, per_device(): lax.all_gather(master_new.astype(jnp.bfloat16), 'dp', axis=0, tiled=True)  297 us
    psum x1, blocking collectives, per_device(): col_total, row_sum = lax.psum((col_part, jnp.sum(row_new)), 'dp')  297 us
    psum x1, blocking collectives, per_device(): energy = lax.psum(jnp.sum(update * update), ('dp', 'mp'))  104 us
  transfers between devices with their start and end apart: 2, of which 2 were waited for; matrix products, arithmetic and copies ran while one was open for 0% of the time, Pallas kernels for 0%

commit v1 on v0

v1 whole, which is shorter than its diff:
```python
import functools

import jax
import jax.numpy as jnp
from jax import lax
from jax.experimental import pallas as pl
from jax.experimental.pallas import tpu as pltpu
from jax.sharding import PartitionSpec as P

MESH = pl.DeviceIdType.MESH
LANES = 128

decay_rate = 0.5
clip_level = 1.0
step_size = 0.5
tiny_term = 1e-30


def kernel(
    ny,
    nk,
    nm,
    splits,
    grad_ref,
    master_ref,
    row_state_ref,
    col_state_ref,
    master_out,
    weight_out,
    row_out,
    col_out,
    parts,
    chunk_sum,
    tile_in,
    extra_in,
    master_rows,
    master_chunk,
    master_tile,
    master_extra,
    stat,
    weights,
    fresh_tile,
    fresh_extra,
    fresh_chunk,
    fresh_rows,
    col_chunk,
    local_sem,
    parts_send,
    parts_recv,
    tile_send,
    tile_recv,
    extra_send,
    extra_recv,
    mrow_send,
    mrow_recv,
    mtile_send,
    mtile_recv,
    mextra_send,
    mextra_recv,
    stat_send,
    stat_recv,
    w_send,
    w_recv,
    wx_send,
    wx_recv,
    f_send,
    f_recv,
    fx_send,
    fx_recv,
    c_send,
    c_recv,
    cx_send,
    cx_recv,
    wout_send,
    wout_recv,
    mout_send,
    mout_recv,
    cout_send,
    cout_recv,
):
    rows = ny * nk
    chunk = chunk_sum.shape[1]
    ff = chunk * nk * nm
    f32 = jnp.float32

    dp = lax.axis_index("dp")
    m = lax.axis_index("mp")
    y = dp // nk
    k = lax.rem(dp, nk)
    heavy = lax.rem(k + (ny // 2) * lax.rem(m, 2), ny)
    is_heavy = heavy == y
    heavy_at = lax.rem(heavy - y + ny, ny)

    def k_of(d):
        return lax.rem(k + d, nk)

    def k_peer(d):
        return (y * nk + k_of(d), m)

    def y_of(d):
        return lax.rem(y + d, ny)

    def y_dev(yy):
        return (yy * nk + k, m)

    def m_peer(d):
        return (dp, lax.rem(m + d, nm))

    def cols(start, width):
        return pl.ds(pl.multiple_of(start, LANES), width)

    def tile(t):
        return cols(t * LANES, LANES)

    def remote(src, dst, send, recv, device):
        return pltpu.make_async_remote_copy(
            src_ref=src, dst_ref=dst, send_sem=send, recv_sem=recv, device_id=device, device_id_type=MESH
        )

    bounds = []
    for s in range(len(splits)):
        first = sum(splits[:s])
        bounds.append((first, splits[s]))

    own = []
    for s, (first, count) in enumerate(bounds):
        c = pltpu.make_async_copy(
            grad_ref.at[:, cols(k * chunk + first * LANES, count * LANES)],
            parts.at[0, :, pl.ds(first * LANES, count * LANES)],
            local_sem.at[s],
        )
        c.start()
        own.append(c)
    own_master = pltpu.make_async_copy(
        master_ref.at[:, cols(k * chunk, chunk)], master_rows.at[k], local_sem.at[len(splits)]
    )
    own_master.start()

    barrier = pltpu.get_barrier_semaphore()
    peers = [k_peer(d) for d in range(1, nk)] + [y_dev(y_of(d)) for d in range(1, ny)] + [m_peer(d) for d in range(1, nm)]
    for device in peers:
        pl.semaphore_signal(barrier, inc=1, device_id=device, device_id_type=MESH)
    pl.semaphore_wait(barrier, len(peers))

    part_copy = {}
    for s, (first, count) in enumerate(bounds):
        for d in range(1, nk):
            c = remote(
                grad_ref.at[:, cols(k_of(d) * chunk + first * LANES, count * LANES)],
                parts.at[d, :, pl.ds(first * LANES, count * LANES)],
                parts_send.at[d, s],
                parts_recv.at[d, s],
                k_peer(d),
            )
            c.start()
            part_copy[d, s] = c
    mrow_copy = {}
    for d in range(1, nk):
        c = remote(
            master_ref.at[:, cols(k_of(d) * chunk, chunk)],
            master_rows.at[k],
            mrow_send.at[d],
            mrow_recv.at[d],
            k_peer(d),
        )
        c.start()
        mrow_copy[d] = c

    def tile_copy(d, t):
        return remote(chunk_sum.at[:, tile(t)], tile_in.at[d], tile_send.at[d], tile_recv.at[d], y_dev(y_of(d)))

    def extra_copy(d, yy):
        return remote(chunk_sum.at[:, pl.ds(ny * LANES, LANES)], extra_in.at[d], extra_send, extra_recv.at[d], y_dev(yy))

    for s, (first, count) in enumerate(bounds):
        where = pl.ds(first * LANES, count * LANES)
        own[s].wait()
        total = parts[0, :, where].astype(f32)
        for d in range(1, nk):
            part_copy[d, s].wait_recv()
            total = total + parts[d, :, where].astype(f32)
        chunk_sum[:, where] = total
        for t in range(first, first + count):
            if t < ny:

                @pl.when(y != t)
                def _():
                    tile_copy(lax.rem(t - y + ny, ny), t).start()
            else:

                @pl.when(jnp.logical_not(is_heavy))
                def _():
                    extra_copy(heavy_at, heavy).start()

    own_master.wait()
    for d in range(1, nk):
        mrow_copy[d].wait_recv()
    for r in range(nk):
        master_chunk[r : r + 1, :] = master_rows[r]
    my_rows = pl.ds(pl.multiple_of(y * nk, nk), nk)
    mtile_copy = {}
    for d in range(1, ny):
        c = remote(
            master_chunk.at[:, tile(y_of(d))],
            master_tile.at[my_rows, :],
            mtile_send.at[d],
            mtile_recv.at[d],
            y_dev(y_of(d)),
        )
        c.start()
        mtile_copy[d] = c
    master_tile[my_rows, :] = master_chunk[:, tile(y)]
    master_last = master_chunk.at[:, pl.ds(ny * LANES, LANES)]

    def mextra_copy(d, yy):
        return remote(master_last, master_extra.at[my_rows, :], mextra_send, mextra_recv.at[d], y_dev(yy))

    @pl.when(jnp.logical_not(is_heavy))
    def _():
        mextra_copy(heavy_at, heavy).start()
        master_extra[...] = jnp.zeros_like(master_extra)
        extra_in[0] = jnp.zeros((rows, LANES), f32)

    @pl.when(is_heavy)
    def _():
        master_extra[my_rows, :] = master_last[...]
        more = chunk_sum[:, pl.ds(ny * LANES, LANES)]
        for d in range(1, ny):
            extra_copy(d, heavy).wait_recv()
            more = more + extra_in[d]
        extra_in[0] = more

    gradient = chunk_sum[:, tile(y)]
    for d in range(1, ny):
        tile_copy(d, y_of(d)).wait_recv()
        gradient = gradient + tile_in[d]
    gradient_x = extra_in[0]

    square = gradient * gradient
    square_x = gradient_x * gradient_x

    def new_col(sq, t):
        state = col_state_ref[:, tile(k * (ny + 1) + t)]
        total = jnp.sum(sq, axis=0, keepdims=True)
        return decay_rate * state + (1.0 - decay_rate) * (total / rows + tiny_term)

    col_new = new_col(square, y)
    col_new_x = new_col(square_x, ny)
    half = gradient * lax.rsqrt(col_new)
    half_x = gradient_x * lax.rsqrt(col_new_x)
    both = jnp.concatenate([square + square_x, half * half + half_x * half_x], axis=0)
    sums = lax.dot_general(
        jnp.ones((8, LANES), f32),
        both,
        (((1,), (1,)), ((), ())),
        precision=lax.Precision.HIGHEST,
        preferred_element_type=f32,
    )

    def exchange(stage, n, peer, value):
        stat[stage, 0] = value
        copies = []
        for d in range(1, n):
            c = remote(
                stat.at[stage, 0], stat.at[stage, d], stat_send.at[stage, d], stat_recv.at[stage, d], peer(d)
            )
            c.start()
            copies.append(c)
        return copies

    def collect(stage, n, copies, value):
        for d in range(1, n):
            copies[d - 1].wait_recv()
            value = value + stat[stage, d]
        return value

    stat_copies = exchange(0, nm, m_peer, sums)
    pending = list(stat_copies)

    col_chunk[:, tile(y)] = col_new
    ccopy = []
    for d in range(1, ny):
        c = remote(col_chunk.at[:, tile(y)], col_chunk.at[:, tile(y)], c_send.at[d], c_recv.at[d], y_dev(y_of(d)))
        c.start()
        ccopy.append(c)

    def cx_copy(d):
        last = col_chunk.at[:, pl.ds(ny * LANES, LANES)]
        return remote(last, last, cx_send.at[d], cx_recv, y_dev(y_of(d)))

    @pl.when(is_heavy)
    def _():
        col_chunk[:, pl.ds(ny * LANES, LANES)] = col_new_x
        for d in range(1, ny):
            cx_copy(d).start()

    sums = collect(0, nm, stat_copies, sums)
    lane = lax.broadcasted_iota(jnp.int32, sums.shape, 1)
    line = lax.broadcasted_iota(jnp.int32, sums.shape, 0)
    state = jnp.where(lane == dp, jnp.broadcast_to(row_state_ref[...], sums.shape), 0.0)
    sums = jnp.where(line == 1, state, sums)
    stat_copies = exchange(1, nk, k_peer, sums)
    pending += stat_copies

    for d in range(1, ny):
        ccopy[d - 1].wait_recv()

    @pl.when(jnp.logical_not(is_heavy))
    def _():
        cx_copy(1).wait_recv()

    col_copies = []
    here = cols(k * chunk, chunk)
    for d in range(1, nk):
        c = remote(col_chunk, col_out.at[:, here], cout_send.at[d], cout_recv.at[d], k_peer(d))
        c.start()
        col_copies.append(c)
    own_col = pltpu.make_async_copy(col_chunk, col_out.at[:, here], local_sem.at[0])
    own_col.start()

    sums = collect(1, nk, stat_copies, sums)
    stat_copies = exchange(2, ny, lambda d: y_dev(y_of(d)), sums)
    pending += stat_copies
    for d in range(1, ny):
        mtile_copy[d].wait_recv()

    @pl.when(is_heavy)
    def _():
        for d in range(1, ny):
            mextra_copy(d, heavy).wait_recv()

    sums = collect(2, ny, stat_copies, sums)

    row_total = sums[0:1, :rows]
    update_total = sums[0:1, rows:]
    row_state = sums[1:2, :rows]
    row_new = decay_rate * row_state + (1.0 - decay_rate) * (row_total / ff + tiny_term)
    mean_row = jnp.sum(row_new, axis=1, keepdims=True) / rows
    energy = mean_row * jnp.sum(update_total / row_new, axis=1, keepdims=True)
    scale = jnp.maximum(1.0, jnp.sqrt(energy / (rows * ff)) / clip_level)
    factor = lax.rsqrt(row_new) * (step_size * jnp.sqrt(mean_row) / scale)
    eye = lax.broadcasted_iota(jnp.int32, (rows, rows), 0) == lax.broadcasted_iota(jnp.int32, (rows, rows), 1)
    factor = jnp.sum(jnp.where(eye, jnp.broadcast_to(factor, (rows, rows)), 0.0), axis=1, keepdims=True)
    fresh = master_tile[...] - factor * half
    fresh_x = master_extra[...] - factor * half_x
    mine = tile(y)
    last = pl.ds(ny * LANES, LANES)
    weights[:, mine] = fresh.astype(jnp.bfloat16)

    wcopy = []
    for d in range(1, ny):
        c = remote(weights.at[:, mine], weights.at[:, mine], w_send.at[d], w_recv.at[d], y_dev(y_of(d)))
        c.start()
        wcopy.append(c)

    def wx_copy(d):
        return remote(weights.at[:, last], weights.at[:, last], wx_send.at[d], wx_recv, y_dev(y_of(d)))

    def rows_of(d):
        return pl.ds(pl.multiple_of(y_of(d) * nk, nk), nk)

    def fx_copy(d):
        return remote(
            fresh_extra.at[rows_of(d), :], fresh_chunk.at[:, last], fx_send.at[d], fx_recv, y_dev(y_of(d))
        )

    @pl.when(is_heavy)
    def _():
        weights[:, last] = fresh_x.astype(jnp.bfloat16)
        for d in range(1, ny):
            wx_copy(d).start()

    fresh_tile[...] = fresh
    fcopy = []
    for d in range(1, ny):
        c = remote(
            fresh_tile.at[rows_of(d), :], fresh_chunk.at[:, mine], f_send.at[d], f_recv.at[d], y_dev(y_of(d))
        )
        c.start()
        fcopy.append(c)
    fresh_chunk[:, mine] = fresh_tile[rows_of(0), :]

    @pl.when(is_heavy)
    def _():
        fresh_extra[...] = fresh_x
        for d in range(1, ny):
            fx_copy(d).start()
        fresh_chunk[:, last] = fresh_extra[rows_of(0), :]

    full_lane = lax.broadcasted_iota(jnp.int32, row_new.shape, 1)
    row_out[...] = jnp.sum(jnp.where(full_lane == dp, row_new, 0.0), axis=1, keepdims=True)

    for d in range(1, ny):
        wcopy[d - 1].wait_recv()

    @pl.when(jnp.logical_not(is_heavy))
    def _():
        wx_copy(1).wait_recv()

    wout = []
    for d in range(1, nk):
        c = remote(weights, weight_out.at[:, here], wout_send.at[d], wout_recv.at[d], k_peer(d))
        c.start()
        wout.append(c)
    own_weight = pltpu.make_async_copy(weights, weight_out.at[:, here], local_sem.at[1])
    own_weight.start()

    for d in range(1, ny):
        fcopy[d - 1].wait_recv()

    @pl.when(jnp.logical_not(is_heavy))
    def _():
        fx_copy(1).wait_recv()

    for r in range(nk):
        fresh_rows[r] = fresh_chunk[r : r + 1, :]
    mout = []
    for d in range(1, nk):
        c = remote(fresh_rows.at[k_of(d)], master_out.at[:, here], mout_send.at[d], mout_recv.at[d], k_peer(d))
        c.start()
        mout.append(c)
    own_fresh = pltpu.make_async_copy(fresh_rows.at[k], master_out.at[:, here], local_sem.at[2])
    own_fresh.start()

    own_col.wait()
    own_weight.wait()
    own_fresh.wait()
    for group in (col_copies, wout, mout):
        for c in group:
            c.wait_recv()
    for c in list(part_copy.values()) + list(mrow_copy.values()) + list(mtile_copy.values()):
        c.wait_send()
    for d in range(1, ny):
        tile_copy(d, y_of(d)).wait_send()
    for group in (pending, ccopy, col_copies, wcopy, fcopy, wout, mout):
        for c in group:
            c.wait_send()

    @pl.when(jnp.logical_not(is_heavy))
    def _():
        extra_copy(heavy_at, heavy).wait_send()
        mextra_copy(heavy_at, heavy).wait_send()

    @pl.when(is_heavy)
    def _():
        for d in range(1, ny):
            cx_copy(d).wait_send()
            wx_copy(d).wait_send()
            fx_copy(d).wait_send()


def build(ny, nk, nm, splits):
    def per_device(grad_partials, master, row_state, col_state):
        grad = grad_partials[0]
        rows, width = grad.shape
        chunk = width // nk
        f32, bf16 = jnp.float32, jnp.bfloat16
        hbm = pl.BlockSpec(memory_space=pl.ANY)
        vmem = pl.BlockSpec(memory_space=pltpu.VMEM)
        dma = pltpu.SemaphoreType.DMA
        pair = lambda *n: [dma(n), dma(n)]
        out = pl.pallas_call(
            functools.partial(kernel, ny, nk, nm, splits),
            out_shape=(
                jax.ShapeDtypeStruct((1, width), f32),
                jax.ShapeDtypeStruct((rows, width), bf16),
                jax.ShapeDtypeStruct((1, 1), f32),
                jax.ShapeDtypeStruct((1, width), f32),
            ),
            in_specs=[hbm, hbm, vmem, vmem],
            out_specs=(hbm, hbm, vmem, hbm),
            scratch_shapes=[
                pltpu.VMEM((nk, rows, chunk), bf16),
                pltpu.VMEM((rows, chunk), f32),
                pltpu.VMEM((ny, rows, LANES), f32),
                pltpu.VMEM((ny, rows, LANES), f32),
                pltpu.VMEM((nk, 1, chunk), f32),
                pltpu.VMEM((nk, chunk), f32),
                pltpu.VMEM((rows, LANES), f32),
                pltpu.VMEM((rows, LANES), f32),
                pltpu.VMEM((3, max(ny, nk, nm), 8, 2 * rows), f32),
                pltpu.VMEM((rows, chunk), bf16),
                pltpu.VMEM((rows, LANES), f32),
                pltpu.VMEM((rows, LANES), f32),
                pltpu.VMEM((nk, chunk), f32),
                pltpu.VMEM((nk, 1, chunk), f32),
                pltpu.VMEM((1, chunk), f32),
                dma((len(splits) + 4,)),
                *pair(nk, len(splits)),
                *pair(ny),
                dma, dma((ny,)),
                *pair(nk),
                *pair(ny),
                dma, dma((ny,)),
                *pair(3, max(ny, nk, nm)),
                *pair(ny),
                dma((ny,)), dma,
                *pair(ny),
                dma((ny,)), dma,
                *pair(ny),
                dma((ny,)), dma,
                *pair(nk),
                *pair(nk),
                *pair(nk),
            ],
            compiler_params=pltpu.CompilerParams(
                collective_id=0, has_side_effects=True, vmem_limit_bytes=32 * 1024 * 1024
            ),
        )(grad, master, row_state.reshape(1, 1), col_state.reshape(1, width))
        master_new, weight_full, row_new, col_new = out
        return (master_new, weight_full, row_new.reshape(1), col_new.reshape(width))

    return per_device


def solution(mesh):
    in_specs = (P("dp", None, "mp"), P("dp", "mp"), P("dp"), P("mp"))
    out_specs = (P("dp", "mp"), P(None, "mp"), P("dp"), P("mp"))
    return jax.shard_map(
        build(8, 8, 8, (3, 3, 3)), mesh=mesh, in_specs=in_specs, out_specs=out_specs, check_vma=False
    )
```

time: 1360 us -> 81.2 us (0.06)
  waiting for transfers between devices: 909 us -> 0 us
  blocking collectives: 416 us -> 0 us
  Pallas kernels: 0 us -> 72.5 us
  between operations: 17.9 us -> 3.04 us
    unnamed x3 -> x0, waiting for transfers between devices: 612 us -> none
    psum x3 -> x0, blocking collectives: 416 us -> none  [the longest x1 297 us: per_device(): col_total, row_sum = lax.psum((col_part, jnp.sum(row_new)), 'dp')]
    all_gather x1 -> x0, waiting for transfers between devices: 297 us -> none  [per_device(): lax.all_gather(master_new.astype(jnp.bfloat16), 'dp', axis=0, tiled=True)]
    pallas_call x0 -> x1, Pallas kernels: none -> 72.5 us  [per_device(): pl.pallas_call(functools.partial(kernel, ny, nk, nm, splits), out_shape=(...]
  transfers between devices with their start and end apart: 2 -> 0, of which waited for: 2 -> 0; matrix products, arithmetic and copies ran while one was open for 0% -> 0% of each run, Pallas kernels for 0% -> 0%
where the time goes in v1:
time: 81.2 us; the launch traced here: 80.5 us
  Pallas kernels  72.5 us (89%)
  local copies, waits for them, and re-layouts  5.05 us (6%)
  between operations  3.04 us (4%)
    pallas_call x1, Pallas kernels, per_device(): pl.pallas_call(functools.partial(kernel, ny, nk, nm, splits), out_shape=(...  72.5 us
    unnamed x9, local copies, waits for them, and re-layouts  5.05 us

profile of v1, /device:TPU:6, one launch (start us, length us, event | category | flops | bytes accessed | tf_op | source)
XLA Modules:
  0.0 80.5 jit_solution(5353195250608713008)
XLA Ops:
  1.3 0.0 copy-start
  1.3 1.3 %copy-done = bf16[1,64,9216]{2,1,0:T(8,128)(2,1)S(1)} copy-done((bf16[1,64,9216]{2,1,0:T(8,128)(2,1)S(1)}, bf16[1,64,9216]{2,1,0:T(8,128)(2,1)}, u32[]{:S(2)}) %copy-start) | copy-done | bytes 1179672
  2.5 0.0 copy-start.1
  2.6 0.8 copy-done.1
  3.3 0.0 copy-start.2
  3.3 0.8 copy-done.2
  4.1 72.5 %shard_map.75 = (f32[1,9216]{1,0:T(1,128)S(1)}, bf16[64,9216]{1,0:T(8,128)(2,1)S(1)}, f32[1,1]{1,0:T(1,128)}, f32[1,9216]{1,0:T(1,128)S(1)}) custom-call(bf16[64,9216]{1,0:T(8,128)(2,1)S(1)} %bitcast.6, f32[1,9216]{1,0:T(1,128)S(1)} %copy-done.1, f32[1,1]{1,0:T(1,128)} %bitcast.5.row_state_ref, f32[1,9216]{1,0:T(1,128)S(1)} %bitcast.7), custom_call_target="tpu_custom_call" | custom-call | tf_op jit(solution)/shard_map/pallas_call | solution.py:462
  76.6 0.6 copy.13
  77.2 1.0 %copy.14 = bf16[64,9216]{1,0:T(8,128)(2,1)} copy(bf16[64,9216]{1,0:T(8,128)(2,1)S(1)} %get-tuple-element.17) | data formatting | bytes 2359296
  78.8 0.6 copy.16
Async XLA Ops:
  1.3 1.3 %copy-start = (bf16[1,64,9216]{2,1,0:T(8,128)(2,1)S(1)}, bf16[1,64,9216]{2,1,0:T(8,128)(2,1)}, u32[]{:S(2)}) copy-start(bf16[1,64,9216]{2,1,0:T(8,128)(2,1)} %param.4) | copy-start | bytes 3538948
  2.5 0.8 copy-start.1
  3.3 0.8 copy-start.2

commit v2 on v0

v2 whole, which is shorter than its diff:
```python
import functools

import jax
import jax.numpy as jnp
from jax import lax
from jax.experimental import pallas as pl
from jax.experimental.pallas import tpu as pltpu
from jax.sharding import PartitionSpec as P

MESH = pl.DeviceIdType.MESH
LANES = 128
F32, BF16 = jnp.float32, jnp.bfloat16

decay_rate = 0.5
clip_level = 1.0
step_size = 0.5
tiny_term = 1e-30


class Slots:
    def __init__(self):
        self.used = 0

    def take(self, n=1):
        self.used += n
        return self.used - n


def kernel(
    n,
    nm,
    splits,
    grad_ref,
    master_ref,
    row_state_ref,
    col_state_ref,
    master_out,
    weight_out,
    row_out,
    col_out,
    parts,
    chunk_sum,
    tile_in,
    extra_in,
    master_rows,
    master_full,
    half_full,
    side_tile,
    side_extra,
    side,
    side_send,
    side_in,
    stat,
    fresh_rows,
    col_chunk,
    col_state,
    local_sem,
    send_sem,
    recv_sem,
):
    rows, chunk = chunk_sum.shape
    ff = chunk * n * nm
    per_chunk = n + 1
    q = side_in.shape[1]
    top = rows - q

    dp = lax.axis_index("dp")
    m = lax.axis_index("mp")
    y = dp // n
    k = lax.rem(dp, n)
    shift = (n // 2) * lax.rem(m, 2)
    heavy = lax.rem(k + shift, n)
    is_heavy = heavy == y
    heavy_at = lax.rem(heavy - y + n, n)

    def chunk_of_extra(yy):
        return lax.rem(yy + shift, n)

    def k_of(d):
        return lax.rem(k + d, n)

    def y_of(d):
        return lax.rem(y + d, n)

    def k_peer(d):
        return (y * n + k_of(d), m)

    def y_dev(yy):
        return (yy * n + k, m)

    def y_peer(d):
        return y_dev(y_of(d))

    def m_peer(d):
        return (dp, lax.rem(m + d, nm))

    def cols(start, width):
        return pl.ds(pl.multiple_of(start, LANES), width)

    def tile(t):
        return cols(t * LANES, LANES)

    slots = Slots()
    sent = []

    def remote(src, dst, slot, device):
        return pltpu.make_async_remote_copy(
            src_ref=src,
            dst_ref=dst,
            send_sem=send_sem.at[slot],
            recv_sem=recv_sem.at[slot],
            device_id=device,
            device_id_type=MESH,
        )

    def start_all(make):
        base = slots.take(n)
        copies = []
        for d in range(1, n):
            c = make(base + d, d)
            c.start()
            copies.append(c)
        sent.extend(copies)
        return copies

    def arrived(copies):
        for c in copies:
            c.wait_recv()

    mine = tile(y)
    last = pl.ds(n * LANES, LANES)
    here = cols(k * chunk, chunk)
    my_rows = pl.ds(pl.multiple_of(y * n, n), n)

    bounds = [(sum(splits[:s]), splits[s]) for s in range(len(splits))]
    own = []
    for s, (first, count) in enumerate(bounds):
        c = pltpu.make_async_copy(
            grad_ref.at[:, cols(k * chunk + first * LANES, count * LANES)],
            parts.at[0, :, pl.ds(first * LANES, count * LANES)],
            local_sem.at[s],
        )
        c.start()
        own.append(c)
    own_master = pltpu.make_async_copy(master_ref.at[:, here], master_rows.at[k], local_sem.at[len(splits)])
    own_master.start()
    own_state = pltpu.make_async_copy(col_state_ref, col_state, local_sem.at[len(splits) + 1])
    own_state.start()

    barrier = pltpu.get_barrier_semaphore()
    peers = [k_peer(d) for d in range(1, n)] + [y_peer(d) for d in range(1, n)] + [m_peer(d) for d in range(1, nm)]
    for device in peers:
        pl.semaphore_signal(barrier, inc=1, device_id=device, device_id_type=MESH)
    pl.semaphore_wait(barrier, len(peers))

    mrow = start_all(
        lambda slot, d: remote(master_ref.at[:, cols(k_of(d) * chunk, chunk)], master_rows.at[k], slot, k_peer(d))
    )
    part = [
        start_all(
            lambda slot, d: remote(
                grad_ref.at[:, cols(k_of(d) * chunk + first * LANES, count * LANES)],
                parts.at[d, :, pl.ds(first * LANES, count * LANES)],
                slot,
                k_peer(d),
            )
        )
        for first, count in bounds
    ]
    own_master.wait()
    arrived(mrow)
    master_full[my_rows, :] = jnp.concatenate([master_rows[r] for r in range(n)], axis=0)
    mfull = start_all(
        lambda slot, d: remote(master_full.at[my_rows, :], master_full.at[my_rows, :], slot, y_peer(d))
    )

    tile_slot = slots.take(n)
    extra_slot = slots.take(n)

    def tile_copy(d, t):
        return remote(chunk_sum.at[:, tile(t)], tile_in.at[d], tile_slot + d, y_peer(d))

    def extra_copy(d):
        return remote(chunk_sum.at[:, last], extra_in.at[d], extra_slot + d, y_dev(heavy))

    for s, (first, count) in enumerate(bounds):
        where = pl.ds(first * LANES, count * LANES)
        own[s].wait()
        total = parts[0, :, where].astype(F32)
        for d in range(1, n):
            part[s][d - 1].wait_recv()
            total = total + parts[d, :, where].astype(F32)
        chunk_sum[:, where] = total
        for t in range(first, first + count):
            if t < n:

                @pl.when(y != t)
                def _():
                    tile_copy(lax.rem(t - y + n, n), t).start()
            else:

                @pl.when(jnp.logical_not(is_heavy))
                def _():
                    extra_copy(heavy_at).start()

    @pl.when(jnp.logical_not(is_heavy))
    def _():
        extra_in[0] = jnp.zeros((rows, LANES), F32)

    gradient = chunk_sum[:, mine]
    for d in range(1, n):
        tile_copy(d, y_of(d)).wait_recv()
        gradient = gradient + tile_in[d]

    @pl.when(is_heavy)
    def _():
        more = chunk_sum[:, last]
        for d in range(1, n):
            extra_copy(d).wait_recv()
            more = more + extra_in[d]
        extra_in[0] = more

    gradient_x = extra_in[0]

    own_state.wait()
    square = gradient * gradient
    square_x = gradient_x * gradient_x

    def new_col(sq, t):
        state = col_state[:, tile(k * per_chunk + t)]
        total = jnp.sum(sq, axis=0, keepdims=True)
        return decay_rate * state + (1.0 - decay_rate) * (total / rows + tiny_term)

    col_new = new_col(square, y)
    col_new_x = new_col(square_x, n)
    half = gradient * lax.rsqrt(col_new)
    half_x = gradient_x * lax.rsqrt(col_new_x)
    both = jnp.concatenate([square + square_x, half * half + half_x * half_x], axis=0)
    sums = lax.dot_general(
        jnp.ones((8, LANES), F32),
        both,
        (((1,), (1,)), ((), ())),
        precision=lax.Precision.HIGHEST,
        preferred_element_type=F32,
    )

    stat_slots = slots.take(3 * max(n, nm))

    def exchange(stage, members, peer, value):
        stat[stage, 0] = value
        copies = []
        for d in range(1, members):
            c = remote(
                stat.at[stage, 0], stat.at[stage, d], stat_slots + stage * max(n, nm) + d, peer(d)
            )
            c.start()
            copies.append(c)
        sent.extend(copies)
        return copies

    def collect(stage, copies, value):
        for d, c in enumerate(copies):
            c.wait_recv()
            value = value + stat[stage, d + 1]
        return value

    stat_copies = exchange(0, nm, m_peer, sums)

    half_full[:, mine] = half
    hcopy = start_all(lambda slot, d: remote(half_full.at[:, mine], half_full.at[:, mine], slot, y_peer(d)))
    hx_send = slots.take(n)
    hx_recv = slots.take()

    def one_to_all(src, dst, send, recv, device):
        return pltpu.make_async_remote_copy(
            src_ref=src,
            dst_ref=dst,
            send_sem=send_sem.at[send],
            recv_sem=recv_sem.at[recv],
            device_id=device,
            device_id_type=MESH,
        )

    def hx_copy(d):
        return one_to_all(half_full.at[:, last], half_full.at[:, last], hx_send + d, hx_recv, y_peer(d))

    @pl.when(is_heavy)
    def _():
        half_full[:, last] = half_x
        for d in range(1, n):
            hx_copy(d).start()

    col_chunk[:, mine] = col_new
    ccopy = start_all(lambda slot, d: remote(col_chunk.at[:, mine], col_chunk.at[:, mine], slot, y_peer(d)))
    cx_send = slots.take(n)
    cx_recv = slots.take()

    def cx_copy(d):
        return one_to_all(col_chunk.at[:, last], col_chunk.at[:, last], cx_send + d, cx_recv, y_peer(d))

    @pl.when(is_heavy)
    def _():
        col_chunk[:, last] = col_new_x
        for d in range(1, n):
            cx_copy(d).start()

    arrived(mfull)
    side_tile[0] = half[top:, :]
    side_tile[1] = master_full[top:, mine]
    scopy = start_all(lambda slot, d: remote(side_tile, side.at[k], slot, k_peer(d)))
    side[k] = side_tile[...]
    sx_send = slots.take(n)
    sx_recv = slots.take()

    def sx_copy(d):
        return one_to_all(side_extra, side.at[n], sx_send + d, sx_recv, k_peer(d))

    @pl.when(is_heavy)
    def _():
        side_extra[0] = half_x[top:, :]
        side_extra[1] = master_full[top:, last]
        for d in range(1, n):
            sx_copy(d).start()
        side[n] = side_extra[...]

    sums = collect(0, stat_copies, sums)
    lane = lax.broadcasted_iota(jnp.int32, sums.shape, 1)
    line = lax.broadcasted_iota(jnp.int32, sums.shape, 0)
    state = jnp.where(lane == dp, jnp.broadcast_to(row_state_ref[...], sums.shape), 0.0)
    sums = jnp.where(line == 1, state, sums)
    stat_copies = exchange(1, n, k_peer, sums)

    arrived(ccopy)

    @pl.when(jnp.logical_not(is_heavy))
    def _():
        cx_copy(1).wait_recv()

    sums = collect(1, stat_copies, sums)
    stat_copies = exchange(2, n, y_peer, sums)

    ocopy = start_all(lambda slot, d: remote(col_chunk, col_out.at[:, here], slot, k_peer(d)))
    col_out[:, here] = col_chunk[...]
    arrived(hcopy)
    arrived(scopy)

    @pl.when(jnp.logical_not(is_heavy))
    def _():
        hx_copy(1).wait_recv()
        sx_copy(1).wait_recv()

    sums = collect(2, stat_copies, sums)

    row_total = sums[0:1, :rows]
    update_total = sums[0:1, rows:]
    row_state = sums[1:2, :rows]
    row_new = decay_rate * row_state + (1.0 - decay_rate) * (row_total / ff + tiny_term)
    mean_row = jnp.sum(row_new, axis=1, keepdims=True) / rows
    energy = mean_row * jnp.sum(update_total / row_new, axis=1, keepdims=True)
    scale = jnp.maximum(1.0, jnp.sqrt(energy / (rows * ff)) / clip_level)
    factor = lax.rsqrt(row_new) * (step_size * jnp.sqrt(mean_row) / scale)
    eye = lax.broadcasted_iota(jnp.int32, (rows, rows), 0) == lax.broadcasted_iota(jnp.int32, (rows, rows), 1)
    factor = jnp.sum(jnp.where(eye, jnp.broadcast_to(factor, (rows, rows)), 0.0), axis=1, keepdims=True)

    for first, count in bounds:
        where = pl.ds(first * LANES, count * LANES)
        fresh = master_full[:top, where] - factor[:top] * half_full[:top, where]
        weight_out[:top, cols(k * chunk + first * LANES, count * LANES)] = fresh.astype(BF16)
    upper = weight_out.at[pl.ds(0, top), here]
    wcopy = start_all(lambda slot, d: remote(upper, upper, slot, k_peer(d)))

    def side_tile_at(j, yy):
        chunk_at = j if j < n else chunk_of_extra(yy)
        return tile(chunk_at * per_chunk + (yy if j < n else n))

    for j in range(per_chunk):
        fresh = (side[j, 1] - factor[top:] * side[j, 0]).astype(BF16)
        side_send[:, pl.ds(j * LANES, LANES)] = fresh
        weight_out[top:, side_tile_at(j, y)] = fresh
    ucopy = start_all(lambda slot, d: remote(side_send, side_in.at[d], slot, y_peer(d)))

    pick = lax.broadcasted_iota(jnp.int32, (n, rows), 1) - y * n == lax.broadcasted_iota(jnp.int32, (n, rows), 0)
    row_factor = lax.rsqrt(row_new) * (step_size * jnp.sqrt(mean_row) / scale)
    row_factor = jnp.sum(jnp.where(pick, jnp.broadcast_to(row_factor, (n, rows)), 0.0), axis=1, keepdims=True)
    fresh = master_full[my_rows, :] - row_factor * half_full[my_rows, :]
    for r in range(n):
        fresh_rows[r] = fresh[r : r + 1, :]
    fcopy = start_all(lambda slot, d: remote(fresh_rows.at[k_of(d)], master_out.at[:, here], slot, k_peer(d)))
    master_out[:, here] = fresh_rows[k]

    full_lane = lax.broadcasted_iota(jnp.int32, row_new.shape, 1)
    row_out[...] = jnp.sum(jnp.where(full_lane == dp, row_new, 0.0), axis=1, keepdims=True)

    for d in range(1, n):
        ucopy[d - 1].wait_recv()
        yy = lax.rem(y - d + n, n)
        for j in range(per_chunk):
            weight_out[top:, side_tile_at(j, yy)] = side_in[d, :, pl.ds(j * LANES, LANES)]
    arrived(ocopy)
    arrived(fcopy)
    arrived(wcopy)

    for c in sent:
        c.wait_send()
    for d in range(1, n):
        tile_copy(d, y_of(d)).wait_send()

    @pl.when(jnp.logical_not(is_heavy))
    def _():
        extra_copy(heavy_at).wait_send()

    @pl.when(is_heavy)
    def _():
        for d in range(1, n):
            hx_copy(d).wait_send()
            cx_copy(d).wait_send()
            sx_copy(d).wait_send()


def build(n, nm, splits):
    def per_device(grad_partials, master, row_state, col_state):
        grad = grad_partials[0]
        rows, width = grad.shape
        chunk = width // n
        quarter = rows // 4
        hbm = pl.BlockSpec(memory_space=pltpu.HBM)
        vmem = pl.BlockSpec(memory_space=pltpu.VMEM)
        dma = pltpu.SemaphoreType.DMA

        def in_hbm(a):
            return pltpu.with_memory_space_constraint(a, pltpu.HBM)

        out = pl.pallas_call(
            functools.partial(kernel, n, nm, splits),
            out_shape=(
                jax.ShapeDtypeStruct((1, width), F32),
                jax.ShapeDtypeStruct((rows, width), BF16),
                jax.ShapeDtypeStruct((1, 1), F32),
                jax.ShapeDtypeStruct((1, width), F32),
            ),
            in_specs=[hbm, hbm, vmem, hbm],
            out_specs=(vmem, vmem, vmem, vmem),
            scratch_shapes=[
                pltpu.VMEM((n, rows, chunk), BF16),
                pltpu.VMEM((rows, chunk), F32),
                pltpu.VMEM((n, rows, LANES), F32),
                pltpu.VMEM((n, rows, LANES), F32),
                pltpu.VMEM((n, 1, chunk), F32),
                pltpu.VMEM((rows, chunk), F32),
                pltpu.VMEM((rows, chunk), F32),
                pltpu.VMEM((2, quarter, LANES), F32),
                pltpu.VMEM((2, quarter, LANES), F32),
                pltpu.VMEM((n + 1, 2, quarter, LANES), F32),
                pltpu.VMEM((quarter, chunk), BF16),
                pltpu.VMEM((n, quarter, chunk), BF16),
                pltpu.VMEM((3, max(n, nm), 8, 2 * rows), F32),
                pltpu.VMEM((n, 1, chunk), F32),
                pltpu.VMEM((1, chunk), F32),
                pltpu.VMEM((1, width), F32),
                dma((len(splits) + 2,)),
                dma((256,)),
                dma((256,)),
            ],
            compiler_params=pltpu.CompilerParams(
                collective_id=0, has_side_effects=True, vmem_limit_bytes=32 * 1024 * 1024
            ),
        )(in_hbm(grad), in_hbm(master), row_state.reshape(1, 1), in_hbm(col_state.reshape(1, width)))
        master_new, weight_full, row_new, col_new = out
        return (master_new, weight_full, row_new.reshape(1), col_new.reshape(width))

    return per_device


def solution(mesh):
    in_specs = (P("dp", None, "mp"), P("dp", "mp"), P("dp"), P("mp"))
    out_specs = (P("dp", "mp"), P(None, "mp"), P("dp"), P("mp"))
    return jax.shard_map(
        build(8, 8, (3, 3, 3)), mesh=mesh, in_specs=in_specs, out_specs=out_specs, check_vma=False
    )
```

time: 1360 us -> 75.5 us (0.06)
  waiting for transfers between devices: 909 us -> 0 us
  blocking collectives: 416 us -> 0 us
  Pallas kernels: 0 us -> 69.5 us
  between operations: 17.9 us -> 2.98 us
    unnamed x3 -> x0, waiting for transfers between devices: 612 us -> none
    psum x3 -> x0, blocking collectives: 416 us -> none  [the longest x1 297 us: per_device(): col_total, row_sum = lax.psum((col_part, jnp.sum(row_new)), 'dp')]
    all_gather x1 -> x0, waiting for transfers between devices: 297 us -> none  [per_device(): lax.all_gather(master_new.astype(jnp.bfloat16), 'dp', axis=0, tiled=True)]
    pallas_call x0 -> x1, Pallas kernels: none -> 69.5 us  [per_device(): pl.pallas_call(functools.partial(kernel, n, nm, splits), out_shape=(jax.S...]
  transfers between devices with their start and end apart: 2 -> 0, of which waited for: 2 -> 0; matrix products, arithmetic and copies ran while one was open for 0% -> 0% of each run, Pallas kernels for 0% -> 0%
where the time goes in v2:
time: 75.5 us; the launch traced here: 74.7 us
  Pallas kernels  69.5 us (92%)
  between operations  2.98 us (4%)
  local copies, waits for them, and re-layouts  2.25 us (3%)
    pallas_call x1, Pallas kernels, per_device(): pl.pallas_call(functools.partial(kernel, n, nm, splits), out_shape=(jax.S...  69.5 us
    unnamed x3, local copies, waits for them, and re-layouts  2.25 us

profile of v2, /device:TPU:6, one launch (start us, length us, event | category | flops | bytes accessed | tf_op | source)
XLA Modules:
  0.0 74.7 jit_solution(9051501999339148033)
XLA Ops:
  1.3 69.5 %shard_map.75 = (f32[1,9216]{1,0:T(1,128)S(1)}, bf16[64,9216]{1,0:T(8,128)(2,1)S(1)}, f32[1,1]{1,0:T(1,128)}, f32[1,9216]{1,0:T(1,128)S(1)}) custom-call(bf16[64,9216]{1,0:T(8,128)(2,1)} %bitcast.7, f32[1,9216]{1,0:T(1,128)} %master_ref.1, f32[1,1]{1,0:T(1,128)} %bitcast.5.row_state_ref, f32[1,9216]{1,0:T(1,128)} %bitcast.8), custom_call_target="tpu_custom_call" | custom-call | tf_op jit(solution)/shard_map/pallas_call | solution.py:433
  70.8 0.6 copy.13
  71.4 1.0 %copy.14 = bf16[64,9216]{1,0:T(8,128)(2,1)} copy(bf16[64,9216]{1,0:T(8,128)(2,1)S(1)} %get-tuple-element.17) | data formatting | bytes 2359296
  73.0 0.6 copy.16

commit v3 on v2

--- a/solution.py
+++ b/solution.py
@@ -113,19 +113,18 @@
             device_id_type=MESH,
         )
 
-    def start_all(make):
-        base = slots.take(n)
-        copies = []
-        for d in range(1, n):
-            c = make(base + d, d)
-            c.start()
-            copies.append(c)
-        sent.extend(copies)
-        return copies
-
-    def arrived(copies):
-        for c in copies:
-            c.wait_recv()
+    def start_all(whole, make):
+        slot = slots.take()
+        for d in range(1, n):
+            make(slot, d).start()
+        group = remote(whole, whole, slot, k_peer(1))
+        sent.append(group)
+        return group
+
+    others = pl.ds(1, n - 1)
+    seven = pl.ds(0, n - 1)
+    seven_tiles = pl.ds(0, (n - 1) * LANES)
+    seven_chunks = pl.ds(0, (n - 1) * chunk)
 
     mine = tile(y)
     last = pl.ds(n * LANES, LANES)
@@ -154,10 +153,12 @@
     pl.semaphore_wait(barrier, len(peers))
 
     mrow = start_all(
+        master_rows.at[seven],
         lambda slot, d: remote(master_ref.at[:, cols(k_of(d) * chunk, chunk)], master_rows.at[k], slot, k_peer(d))
     )
     part = [
         start_all(
+            parts.at[others, :, pl.ds(first * LANES, count * LANES)],
             lambda slot, d: remote(
                 grad_ref.at[:, cols(k_of(d) * chunk + first * LANES, count * LANES)],
                 parts.at[d, :, pl.ds(first * LANES, count * LANES)],
@@ -168,27 +169,30 @@
         for first, count in bounds
     ]
     own_master.wait()
-    arrived(mrow)
+    mrow.wait_recv()
     master_full[my_rows, :] = jnp.concatenate([master_rows[r] for r in range(n)], axis=0)
     mfull = start_all(
+        master_full.at[pl.ds(0, rows - n), :],
         lambda slot, d: remote(master_full.at[my_rows, :], master_full.at[my_rows, :], slot, y_peer(d))
     )
 
-    tile_slot = slots.take(n)
-    extra_slot = slots.take(n)
+    tile_slot = slots.take()
+    extra_slot = slots.take()
+    tiles_in = remote(tile_in.at[others], tile_in.at[others], tile_slot, k_peer(1))
+    extras_in = remote(extra_in.at[others], extra_in.at[others], extra_slot, k_peer(1))
 
     def tile_copy(d, t):
-        return remote(chunk_sum.at[:, tile(t)], tile_in.at[d], tile_slot + d, y_peer(d))
+        return remote(chunk_sum.at[:, tile(t)], tile_in.at[d], tile_slot, y_peer(d))
 
     def extra_copy(d):
-        return remote(chunk_sum.at[:, last], extra_in.at[d], extra_slot + d, y_dev(heavy))
+        return remote(chunk_sum.at[:, last], extra_in.at[d], extra_slot, y_dev(heavy))
 
     for s, (first, count) in enumerate(bounds):
         where = pl.ds(first * LANES, count * LANES)
         own[s].wait()
+        part[s].wait_recv()
         total = parts[0, :, where].astype(F32)
         for d in range(1, n):
-            part[s][d - 1].wait_recv()
             total = total + parts[d, :, where].astype(F32)
         chunk_sum[:, where] = total
         for t in range(first, first + count):
@@ -207,16 +211,16 @@
     def _():
         extra_in[0] = jnp.zeros((rows, LANES), F32)
 
+    tiles_in.wait_recv()
     gradient = chunk_sum[:, mine]
     for d in range(1, n):
-        tile_copy(d, y_of(d)).wait_recv()
         gradient = gradient + tile_in[d]
 
     @pl.when(is_heavy)
     def _():
+        extras_in.wait_recv()
         more = chunk_sum[:, last]
         for d in range(1, n):
-            extra_copy(d).wait_recv()
             more = more + extra_in[d]
         extra_in[0] = more
 
@@ -244,112 +248,106 @@
         preferred_element_type=F32,
     )
 
-    stat_slots = slots.take(3 * max(n, nm))
-
     def exchange(stage, members, peer, value):
         stat[stage, 0] = value
-        copies = []
+        slot = slots.take()
         for d in range(1, members):
-            c = remote(
-                stat.at[stage, 0], stat.at[stage, d], stat_slots + stage * max(n, nm) + d, peer(d)
-            )
-            c.start()
-            copies.append(c)
-        sent.extend(copies)
-        return copies
-
-    def collect(stage, copies, value):
-        for d, c in enumerate(copies):
-            c.wait_recv()
-            value = value + stat[stage, d + 1]
+            remote(stat.at[stage, 0], stat.at[stage, d], slot, peer(d)).start()
+        if members == 1:
+            return None
+        whole = stat.at[stage, pl.ds(1, members - 1)]
+        group = remote(whole, whole, slot, k_peer(1))
+        sent.append(group)
+        return group
+
+    def collect(stage, members, group, value):
+        if group is not None:
+            group.wait_recv()
+        for d in range(1, members):
+            value = value + stat[stage, d]
         return value
 
-    stat_copies = exchange(0, nm, m_peer, sums)
+    lane = lax.broadcasted_iota(jnp.int32, sums.shape, 1)
+    line = lax.broadcasted_iota(jnp.int32, sums.shape, 0)
+    state = jnp.where((lane == dp) & (m == 0), jnp.broadcast_to(row_state_ref[...], sums.shape), 0.0)
+    sums = jnp.where(line == 1, state, sums)
+    stat_group = exchange(0, n, y_peer, sums)
 
     half_full[:, mine] = half
-    hcopy = start_all(lambda slot, d: remote(half_full.at[:, mine], half_full.at[:, mine], slot, y_peer(d)))
-    hx_send = slots.take(n)
-    hx_recv = slots.take()
-
-    def one_to_all(src, dst, send, recv, device):
-        return pltpu.make_async_remote_copy(
-            src_ref=src,
-            dst_ref=dst,
-            send_sem=send_sem.at[send],
-            recv_sem=recv_sem.at[recv],
-            device_id=device,
-            device_id_type=MESH,
-        )
-
-    def hx_copy(d):
-        return one_to_all(half_full.at[:, last], half_full.at[:, last], hx_send + d, hx_recv, y_peer(d))
+    half_mine = half_full.at[:, mine]
+    half_last = half_full.at[:, last]
+    h_slot = slots.take()
+    hx_slot = slots.take()
+    hcopy = remote(half_full.at[:, seven_tiles], half_full.at[:, seven_tiles], h_slot, y_peer(1))
+    sent.append(hcopy)
 
     @pl.when(is_heavy)
     def _():
         half_full[:, last] = half_x
-        for d in range(1, n):
-            hx_copy(d).start()
 
     col_chunk[:, mine] = col_new
-    ccopy = start_all(lambda slot, d: remote(col_chunk.at[:, mine], col_chunk.at[:, mine], slot, y_peer(d)))
-    cx_send = slots.take(n)
-    cx_recv = slots.take()
-
-    def cx_copy(d):
-        return one_to_all(col_chunk.at[:, last], col_chunk.at[:, last], cx_send + d, cx_recv, y_peer(d))
+    ccopy = start_all(
+        col_chunk.at[:, seven_tiles],
+        lambda slot, d: remote(col_chunk.at[:, mine], col_chunk.at[:, mine], slot, y_peer(d)),
+    )
+    col_last = col_chunk.at[:, last]
+    cx_slot = slots.take()
 
     @pl.when(is_heavy)
     def _():
         col_chunk[:, last] = col_new_x
         for d in range(1, n):
-            cx_copy(d).start()
-
-    arrived(mfull)
+            remote(col_last, col_last, cx_slot, y_peer(d)).start()
+
+    mfull.wait_recv()
     side_tile[0] = half[top:, :]
     side_tile[1] = master_full[top:, mine]
-    scopy = start_all(lambda slot, d: remote(side_tile, side.at[k], slot, k_peer(d)))
+    scopy = start_all(side.at[seven], lambda slot, d: remote(side_tile, side.at[k], slot, k_peer(d)))
     side[k] = side_tile[...]
-    sx_send = slots.take(n)
-    sx_recv = slots.take()
-
-    def sx_copy(d):
-        return one_to_all(side_extra, side.at[n], sx_send + d, sx_recv, k_peer(d))
+    sx_slot = slots.take()
 
     @pl.when(is_heavy)
     def _():
         side_extra[0] = half_x[top:, :]
         side_extra[1] = master_full[top:, last]
         for d in range(1, n):
-            sx_copy(d).start()
+            remote(side_extra, side.at[n], sx_slot, k_peer(d)).start()
         side[n] = side_extra[...]
 
-    sums = collect(0, stat_copies, sums)
-    lane = lax.broadcasted_iota(jnp.int32, sums.shape, 1)
-    line = lax.broadcasted_iota(jnp.int32, sums.shape, 0)
-    state = jnp.where(lane == dp, jnp.broadcast_to(row_state_ref[...], sums.shape), 0.0)
-    sums = jnp.where(line == 1, state, sums)
-    stat_copies = exchange(1, n, k_peer, sums)
-
-    arrived(ccopy)
+    sums = collect(0, n, stat_group, sums)
+    stat_group = exchange(1, nm, m_peer, sums)
+    for d in range(1, n):
+        remote(half_mine, half_mine, h_slot, y_peer(d)).start()
+
+    @pl.when(is_heavy)
+    def _():
+        for d in range(1, n):
+            remote(half_last, half_last, hx_slot, y_peer(d)).start()
+
+
+    ccopy.wait_recv()
 
     @pl.when(jnp.logical_not(is_heavy))
     def _():
-        cx_copy(1).wait_recv()
-
-    sums = collect(1, stat_copies, sums)
-    stat_copies = exchange(2, n, y_peer, sums)
-
-    ocopy = start_all(lambda slot, d: remote(col_chunk, col_out.at[:, here], slot, k_peer(d)))
+        remote(col_last, col_last, cx_slot, y_peer(1)).wait_recv()
+
+    ocopy = start_all(
+        col_out.at[:, seven_chunks],
+        lambda slot, d: remote(col_chunk, col_out.at[:, here], slot, k_peer(d)),
+    )
     col_out[:, here] = col_chunk[...]
-    arrived(hcopy)
-    arrived(scopy)
+    sums = collect(1, nm, stat_group, sums)
+    stat_group = exchange(2, n, k_peer, sums)
+
+    hcopy.wait_recv()
+    scopy.wait_recv()
 
     @pl.when(jnp.logical_not(is_heavy))
     def _():
-        hx_copy(1).wait_recv()
-        sx_copy(1).wait_recv()
-
-    sums = collect(2, stat_copies, sums)
+        remote(half_last, half_last, hx_slot, y_peer(1)).wait_recv()
+        remote(side_extra, side_extra, sx_slot, k_peer(1)).wait_recv()
+
+    sums = collect(2, n, stat_group, sums)
 
     row_total = sums[0:1, :rows]
     update_total = sums[0:1, rows:]
@@ -367,7 +365,7 @@
         fresh = master_full[:top, where] - factor[:top] * half_full[:top, where]
         weight_out[:top, cols(k * chunk + first * LANES, count * LANES)] = fresh.astype(BF16)
     upper = weight_out.at[pl.ds(0, top), here]
-    wcopy = start_all(lambda slot, d: remote(upper, upper, slot, k_peer(d)))
+    wcopy = start_all(weight_out.at[pl.ds(0, top), seven_chunks], lambda slot, d: remote(upper, upper, slot, k_peer(d)))
 
     def side_tile_at(j, yy):
         chunk_at = j if j < n else chunk_of_extra(yy)
@@ -377,7 +375,7 @@
         fresh = (side[j, 1] - factor[top:] * side[j, 0]).astype(BF16)
         side_send[:, pl.ds(j * LANES, LANES)] = fresh
         weight_out[top:, side_tile_at(j, y)] = fresh
-    ucopy = start_all(lambda slot, d: remote(side_send, side_in.at[d], slot, y_peer(d)))
+    ucopy = start_all(side_in.at[others], lambda slot, d: remote(side_send, side_in.at[d], slot, y_peer(d)))
 
     pick = lax.broadcasted_iota(jnp.int32, (n, rows), 1) - y * n == lax.broadcasted_iota(jnp.int32, (n, rows), 0)
     row_factor = lax.rsqrt(row_new) * (step_size * jnp.sqrt(mean_row) / scale)
@@ -385,25 +383,24 @@
     fresh = master_full[my_rows, :] - row_factor * half_full[my_rows, :]
     for r in range(n):
         fresh_rows[r] = fresh[r : r + 1, :]
-    fcopy = start_all(lambda slot, d: remote(fresh_rows.at[k_of(d)], master_out.at[:, here], slot, k_peer(d)))
+    fcopy = start_all(master_out.at[:, seven_chunks], lambda slot, d: remote(fresh_rows.at[k_of(d)], master_out.at[:, here], slot, k_peer(d)))
     master_out[:, here] = fresh_rows[k]
 
     full_lane = lax.broadcasted_iota(jnp.int32, row_new.shape, 1)
     row_out[...] = jnp.sum(jnp.where(full_lane == dp, row_new, 0.0), axis=1, keepdims=True)
 
+    ucopy.wait_recv()
     for d in range(1, n):
-        ucopy[d - 1].wait_recv()
         yy = lax.rem(y - d + n, n)
         for j in range(per_chunk):
             weight_out[top:, side_tile_at(j, yy)] = side_in[d, :, pl.ds(j * LANES, LANES)]
-    arrived(ocopy)
-    arrived(fcopy)
-    arrived(wcopy)
-
-    for c in sent:
-        c.wait_send()
-    for d in range(1, n):
-        tile_copy(d, y_of(d)).wait_send()
+    ocopy.wait_recv()
+    fcopy.wait_recv()
+    wcopy.wait_recv()
+
+    for group in sent:
+        group.wait_send()
+    tiles_in.wait_send()
 
     @pl.when(jnp.logical_not(is_heavy))
     def _():
@@ -411,10 +408,19 @@
 
     @pl.when(is_heavy)
     def _():
-        for d in range(1, n):
-            hx_copy(d).wait_send()
-            cx_copy(d).wait_send()
-            sx_copy(d).wait_send()
+        remote(half_full.at[:, seven_tiles], half_full.at[:, seven_tiles], hx_slot, y_peer(1)).wait_send()
+        remote(col_chunk.at[:, seven_tiles], col_chunk.at[:, seven_tiles], cx_slot, y_peer(1)).wait_send()
+        remote(side.at[seven], side.at[seven], sx_slot, k_peer(1)).wait_send()
+
+
+def writer(*refs):
+    *pairs, sem = refs
+    count = len(pairs) // 2
+    copies = [pltpu.make_async_copy(pairs[i], pairs[count + i], sem.at[i]) for i in range(count)]
+    for c in copies:
+        c.start()
+    for c in copies:
+        c.wait()
 
 
 def build(n, nm, splits):
@@ -458,14 +464,21 @@
                 pltpu.VMEM((1, chunk), F32),
                 pltpu.VMEM((1, width), F32),
                 dma((len(splits) + 2,)),
-                dma((256,)),
-                dma((256,)),
+                dma((24,)),
+                dma((24,)),
             ],
             compiler_params=pltpu.CompilerParams(
                 collective_id=0, has_side_effects=True, vmem_limit_bytes=32 * 1024 * 1024
             ),
         )(in_hbm(grad), in_hbm(master), row_state.reshape(1, 1), in_hbm(col_state.reshape(1, width)))
-        master_new, weight_full, row_new, col_new = out
+        master_new, weight_full, row_new, col_new = pl.pallas_call(
+            writer,
+            out_shape=tuple(jax.ShapeDtypeStruct(a.shape, a.dtype) for a in out),
+            in_specs=[pl.BlockSpec(memory_space=pl.ANY)] * len(out),
+            out_specs=tuple([hbm] * len(out)),
+            scratch_shapes=[dma((len(out),))],
+            compiler_params=pltpu.CompilerParams(vmem_limit_bytes=1024 * 1024),
+        )(*out)
         return (master_new, weight_full, row_new.reshape(1), col_new.reshape(width))
 
     return per_device
@@ -475,5 +488,5 @@
     in_specs = (P("dp", None, "mp"), P("dp", "mp"), P("dp"), P("mp"))
     out_specs = (P("dp", "mp"), P(None, "mp"), P("dp"), P("mp"))
     return jax.shard_map(
-        build(8, 8, (3, 3, 3)), mesh=mesh, in_specs=in_specs, out_specs=out_specs, check_vma=False
-    )
+        build(8, 8, (4, 4, 1)), mesh=mesh, in_specs=in_specs, out_specs=out_specs, check_vma=False
+    )

time: 75.5 us -> 68.5 us (0.907)
  the two profiles are of different devices: /device:TPU:6 before, /device:TPU:1 now
where the time goes in v3:
time: 68.5 us; the launch traced here: 68.4 us
  Pallas kernels  67.1 us (98%)
  between operations  1.29 us (2%)
    pallas_call x1, Pallas kernels, per_device(): pl.pallas_call(functools.partial(kernel, n, nm, splits), out_shape=(jax.S...  65.4 us
    pallas_call x1, Pallas kernels, per_device(): pl.pallas_call(writer, out_shape=tuple((jax.ShapeDtypeStruct(a.shape, a.d...  1.7 us

profile of v3, /device:TPU:1, one launch (start us, length us, event | category | flops | bytes accessed | tf_op | source)
XLA Modules:
  0.0 68.4 jit_solution(15592150200080147897)
XLA Ops:
  1.3 65.4 %shard_map.75 = (f32[1,9216]{1,0:T(1,128)S(1)}, bf16[64,9216]{1,0:T(8,128)(2,1)S(1)}, f32[1,1]{1,0:T(1,128)}, f32[1,9216]{1,0:T(1,128)S(1)}) custom-call(bf16[64,9216]{1,0:T(8,128)(2,1)} %bitcast.6, f32[1,9216]{1,0:T(1,128)} %master_ref.1, f32[1,1]{1,0:T(1,128)} %bitcast.5.row_state_ref, f32[1,9216]{1,0:T(1,128)} %bitcast.7), custom_call_target="tpu_custom_call" | custom-call | tf_op jit(solution)/shard_map/pallas_call | solution.py:439
  66.7 1.7 %shard_map.76 = (f32[1,9216]{1,0:T(1,128)}, bf16[64,9216]{1,0:T(8,128)(2,1)}, f32[1,1]{1,0:T(1,128)}, f32[1,9216]{1,0:T(1,128)}) custom-call(f32[1,9216]{1,0:T(1,128)S(1)} %get-tuple-element.12.refs_0_, bf16[64,9216]{1,0:T(8,128)(2,1)S(1)} %get-tuple-element.13.refs_1_, f32[1,1]{1,0:T(1,128)} %get-tuple-element.14.refs_2_, ...), custom_call_target="tpu_custom_call" | custom-call | tf_op jit(solution)/shard_map/pallas_call | solution.py:474

commit v4 on v3

--- a/solution.py
+++ b/solution.py
@@ -41,6 +41,8 @@
     parts,
     chunk_sum,
     tile_in,
+    extra_parts,
+    extra_sum,
     extra_in,
     master_rows,
     master_full,
@@ -69,12 +71,14 @@
     y = dp // n
     k = lax.rem(dp, n)
     shift = (n // 2) * lax.rem(m, 2)
-    heavy = lax.rem(k + shift, n)
-    is_heavy = heavy == y
-    heavy_at = lax.rem(heavy - y + n, n)
+    is_heavy = lax.rem(k + shift, n) == y
 
     def chunk_of_extra(yy):
         return lax.rem(yy + shift, n)
+
+    y_top = top // n
+    lower = y >= y_top
+    heavy_at = lax.rem(chunk_of_extra(y) - k + n, n)
 
     def k_of(d):
         return lax.rem(k + d, n)
@@ -121,7 +125,11 @@
         sent.append(group)
         return group
 
+    def whole_of(ref, slot):
+        return remote(ref, ref, slot, k_peer(1))
+
     others = pl.ds(1, n - 1)
+    body = pl.ds(0, n * LANES)
     seven = pl.ds(0, n - 1)
     seven_tiles = pl.ds(0, (n - 1) * LANES)
     seven_chunks = pl.ds(0, (n - 1) * chunk)
@@ -130,6 +138,9 @@
     last = pl.ds(n * LANES, LANES)
     here = cols(k * chunk, chunk)
     my_rows = pl.ds(pl.multiple_of(y * n, n), n)
+
+    def extra_cols(yy):
+        return tile(chunk_of_extra(yy) * per_chunk + n)
 
     bounds = [(sum(splits[:s]), splits[s]) for s in range(len(splits))]
     own = []
@@ -141,6 +152,10 @@
         )
         c.start()
         own.append(c)
+    own_extra = pltpu.make_async_copy(
+        grad_ref.at[:, extra_cols(y)], extra_parts.at[0], local_sem.at[len(splits) + 2]
+    )
+    own_extra.start()
     own_master = pltpu.make_async_copy(master_ref.at[:, here], master_rows.at[k], local_sem.at[len(splits)])
     own_master.start()
     own_state = pltpu.make_async_copy(col_state_ref, col_state, local_sem.at[len(splits) + 1])
@@ -152,40 +167,64 @@
         pl.semaphore_signal(barrier, inc=1, device_id=device, device_id_type=MESH)
     pl.semaphore_wait(barrier, len(peers))
 
-    mrow = start_all(
-        master_rows.at[seven],
-        lambda slot, d: remote(master_ref.at[:, cols(k_of(d) * chunk, chunk)], master_rows.at[k], slot, k_peer(d))
-    )
-    part = [
-        start_all(
+    def part_group(first, count):
+        return start_all(
             parts.at[others, :, pl.ds(first * LANES, count * LANES)],
             lambda slot, d: remote(
                 grad_ref.at[:, cols(k_of(d) * chunk + first * LANES, count * LANES)],
                 parts.at[d, :, pl.ds(first * LANES, count * LANES)],
                 slot,
                 k_peer(d),
-            )
+            ),
         )
-        for first, count in bounds
-    ]
+
+    mrow = start_all(
+        master_rows.at[seven],
+        lambda slot, d: remote(master_ref.at[:, cols(k_of(d) * chunk, chunk)], master_rows.at[k], slot, k_peer(d))
+    )
+    part = [part_group(*bounds[0])]
+    extra_group = start_all(
+        extra_parts.at[others],
+        lambda slot, d: remote(grad_ref.at[:, extra_cols(y_of(d))], extra_parts.at[d], slot, y_peer(d)),
+    )
+    part += [part_group(*b) for b in bounds[1:]]
     own_master.wait()
     mrow.wait_recv()
     master_full[my_rows, :] = jnp.concatenate([master_rows[r] for r in range(n)], axis=0)
-    mfull = start_all(
-        master_full.at[pl.ds(0, rows - n), :],
-        lambda slot, d: remote(master_full.at[my_rows, :], master_full.at[my_rows, :], slot, y_peer(d))
-    )
+    m_slot, mp_slot, mx_slot = slots.take(), slots.take(), slots.take()
+
+    def master_copy(where, slot, device):
+        part = master_full.at[my_rows, where]
+        return remote(part, part, slot, device)
+
+    @pl.when(jnp.logical_not(lower))
+    def _():
+        for d in range(1, n):
+            master_copy(body, m_slot, y_peer(d)).start()
+
+    @pl.when(lower)
+    def _():
+        for d in range(1, n):
+            master_copy(tile(y_of(d)), mp_slot, y_peer(d)).start()
+
+    @pl.when(jnp.logical_not(is_heavy))
+    def _():
+        master_copy(last, mx_slot, y_dev(lax.rem(k + shift, n))).start()
+
+    def master_whole(count, where, slot):
+        return whole_of(master_full.at[pl.ds(0, count * n), where], slot)
 
     tile_slot = slots.take()
     extra_slot = slots.take()
     tiles_in = remote(tile_in.at[others], tile_in.at[others], tile_slot, k_peer(1))
+    extras_whole = extra_in.at[pl.ds(0, 2 * (n - 1))]
     extras_in = remote(extra_in.at[others], extra_in.at[others], extra_slot, k_peer(1))
 
     def tile_copy(d, t):
         return remote(chunk_sum.at[:, tile(t)], tile_in.at[d], tile_slot, y_peer(d))
 
     def extra_copy(d):
-        return remote(chunk_sum.at[:, last], extra_in.at[d], extra_slot, y_dev(heavy))
+        return remote(extra_sum, extra_in.at[d], extra_slot, k_peer(d))
 
     for s, (first, count) in enumerate(bounds):
         where = pl.ds(first * LANES, count * LANES)
@@ -196,16 +235,22 @@
             total = total + parts[d, :, where].astype(F32)
         chunk_sum[:, where] = total
         for t in range(first, first + count):
-            if t < n:
-
-                @pl.when(y != t)
-                def _():
-                    tile_copy(lax.rem(t - y + n, n), t).start()
-            else:
-
-                @pl.when(jnp.logical_not(is_heavy))
-                def _():
-                    extra_copy(heavy_at).start()
+
+            @pl.when(y != t)
+            def _():
+                tile_copy(lax.rem(t - y + n, n), t).start()
+
+        if s == 0:
+            own_extra.wait()
+            extra_group.wait_recv()
+            total = extra_parts[0].astype(F32)
+            for d in range(1, n):
+                total = total + extra_parts[d].astype(F32)
+            extra_sum[...] = total
+
+            @pl.when(jnp.logical_not(is_heavy))
+            def _():
+                extra_copy(heavy_at).start()
 
     @pl.when(jnp.logical_not(is_heavy))
     def _():
@@ -219,7 +264,7 @@
     @pl.when(is_heavy)
     def _():
         extras_in.wait_recv()
-        more = chunk_sum[:, last]
+        more = extra_sum[...]
         for d in range(1, n):
             more = more + extra_in[d]
         extra_in[0] = more
@@ -274,12 +319,15 @@
     stat_group = exchange(0, n, y_peer, sums)
 
     half_full[:, mine] = half
-    half_mine = half_full.at[:, mine]
-    half_last = half_full.at[:, last]
-    h_slot = slots.take()
-    hx_slot = slots.take()
-    hcopy = remote(half_full.at[:, seven_tiles], half_full.at[:, seven_tiles], h_slot, y_peer(1))
-    sent.append(hcopy)
+    half_last = half_full.at[my_rows, last]
+    h_slot, hl_slot, hx_slot = slots.take(), slots.take(), slots.take()
+
+    def half_copy(count, slot, d):
+        part = half_full.at[pl.ds(0, count), mine]
+        return remote(part, part, slot, y_peer(d))
+
+    def half_whole(tiles, count, slot):
+        return whole_of(half_full.at[pl.ds(0, count), pl.ds(0, tiles * LANES)], slot)
 
     @pl.when(is_heavy)
     def _():
@@ -299,7 +347,21 @@
         for d in range(1, n):
             remote(col_last, col_last, cx_slot, y_peer(d)).start()
 
-    mfull.wait_recv()
+    @pl.when(jnp.logical_not(lower))
+    def _():
+        master_whole(y_top - 1, body, m_slot).wait_recv()
+        master_whole(n - y_top, last, mp_slot).wait_recv()
+
+    @pl.when(lower)
+    def _():
+        master_whole(y_top, body, m_slot).wait_recv()
+        if n - y_top > 1:
+            master_whole(n - y_top - 1, last, mp_slot).wait_recv()
+
+    @pl.when(is_heavy)
+    def _():
+        master_whole(n - 1, last, mx_slot).wait_recv()
+
     side_tile[0] = half[top:, :]
     side_tile[1] = master_full[top:, mine]
     scopy = start_all(side.at[seven], lambda slot, d: remote(side_tile, side.at[k], slot, k_peer(d)))
@@ -308,22 +370,28 @@
 
     @pl.when(is_heavy)
     def _():
-        side_extra[0] = half_x[top:, :]
-        side_extra[1] = master_full[top:, last]
-        for d in range(1, n):
-            remote(side_extra, side.at[n], sx_slot, k_peer(d)).start()
-        side[n] = side_extra[...]
+        side_extra[0] = half_x
+        side_extra[1] = master_full[:, last]
+        for d in range(1, n):
+            remote(side_extra, side_extra, sx_slot, k_peer(d)).start()
 
     sums = collect(0, n, stat_group, sums)
     stat_group = exchange(1, nm, m_peer, sums)
     for d in range(1, n):
-        remote(half_mine, half_mine, h_slot, y_peer(d)).start()
-
-    @pl.when(is_heavy)
-    def _():
-        for d in range(1, n):
-            remote(half_last, half_last, hx_slot, y_peer(d)).start()
-
+
+        @pl.when(y_of(d) < y_top)
+        def _():
+            half_copy(top, h_slot, d).start()
+
+        @pl.when(y_of(d) >= y_top)
+        def _():
+            half_copy(rows, hl_slot, d).start()
+
+    @pl.when(is_heavy)
+    def _():
+        for d in range(1, n):
+            part = half_full.at[pl.ds(pl.multiple_of(y_of(d) * n, n), n), last]
+            remote(part, part, hx_slot, y_peer(d)).start()
 
     ccopy.wait_recv()
 
@@ -339,7 +407,14 @@
     sums = collect(1, nm, stat_group, sums)
     stat_group = exchange(2, n, k_peer, sums)
 
-    hcopy.wait_recv()
+    @pl.when(jnp.logical_not(lower))
+    def _():
+        half_whole(n - 1, top, h_slot).wait_recv()
+
+    @pl.when(lower)
+    def _():
+        half_whole(n - 1, rows, hl_slot).wait_recv()
+
     scopy.wait_recv()
 
     @pl.when(jnp.logical_not(is_heavy))
@@ -364,14 +439,17 @@
         where = pl.ds(first * LANES, count * LANES)
         fresh = master_full[:top, where] - factor[:top] * half_full[:top, where]
         weight_out[:top, cols(k * chunk + first * LANES, count * LANES)] = fresh.astype(BF16)
-    upper = weight_out.at[pl.ds(0, top), here]
-    wcopy = start_all(weight_out.at[pl.ds(0, top), seven_chunks], lambda slot, d: remote(upper, upper, slot, k_peer(d)))
+    upper = weight_out.at[pl.ds(0, top), cols(k * chunk, n * LANES)]
+    wcopy = start_all(weight_out.at[pl.ds(0, top), pl.ds(0, (n - 1) * n * LANES)], lambda slot, d: remote(upper, upper, slot, k_peer(d)))
+
+    weight_out[:, extra_cols(y)] = (side_extra[1] - factor * side_extra[0]).astype(BF16)
+    extra_out = weight_out.at[:, extra_cols(y)]
+    xcopy = start_all(weight_out.at[:, seven_tiles], lambda slot, d: remote(extra_out, extra_out, slot, y_peer(d)))
 
     def side_tile_at(j, yy):
-        chunk_at = j if j < n else chunk_of_extra(yy)
-        return tile(chunk_at * per_chunk + (yy if j < n else n))
-
-    for j in range(per_chunk):
+        return tile(j * per_chunk + yy)
+
+    for j in range(n):
         fresh = (side[j, 1] - factor[top:] * side[j, 0]).astype(BF16)
         side_send[:, pl.ds(j * LANES, LANES)] = fresh
         weight_out[top:, side_tile_at(j, y)] = fresh
@@ -392,25 +470,43 @@
     ucopy.wait_recv()
     for d in range(1, n):
         yy = lax.rem(y - d + n, n)
-        for j in range(per_chunk):
+        for j in range(n):
             weight_out[top:, side_tile_at(j, yy)] = side_in[d, :, pl.ds(j * LANES, LANES)]
     ocopy.wait_recv()
     fcopy.wait_recv()
+    xcopy.wait_recv()
     wcopy.wait_recv()
 
     for group in sent:
         group.wait_send()
     tiles_in.wait_send()
 
+    @pl.when(jnp.logical_not(lower))
+    def _():
+        master_whole(n - 1, body, m_slot).wait_send()
+        half_whole(y_top - 1, top, h_slot).wait_send()
+        half_whole(n - y_top, rows, hl_slot).wait_send()
+
+    @pl.when(lower)
+    def _():
+        master_whole(n - 1, last, mp_slot).wait_send()
+        half_whole(y_top, top, h_slot).wait_send()
+        if n - y_top > 1:
+            half_whole(n - y_top - 1, rows, hl_slot).wait_send()
+
     @pl.when(jnp.logical_not(is_heavy))
     def _():
+        master_copy(last, mx_slot, y_peer(1)).wait_send()
+
+    @pl.when(jnp.logical_not(is_heavy))
+    def _():
         extra_copy(heavy_at).wait_send()
 
     @pl.when(is_heavy)
     def _():
-        remote(half_full.at[:, seven_tiles], half_full.at[:, seven_tiles], hx_slot, y_peer(1)).wait_send()
+        whole_of(half_full.at[pl.ds(0, n), seven_tiles], hx_slot).wait_send()
         remote(col_chunk.at[:, seven_tiles], col_chunk.at[:, seven_tiles], cx_slot, y_peer(1)).wait_send()
-        remote(side.at[seven], side.at[seven], sx_slot, k_peer(1)).wait_send()
+        remote(extras_whole, extras_whole, sx_slot, k_peer(1)).wait_send()
 
 
 def writer(*refs):
@@ -450,22 +546,24 @@
                 pltpu.VMEM((n, rows, chunk), BF16),
                 pltpu.VMEM((rows, chunk), F32),
                 pltpu.VMEM((n, rows, LANES), F32),
-                pltpu.VMEM((n, rows, LANES), F32),
+                pltpu.VMEM((n, rows, LANES), BF16),
+                pltpu.VMEM((rows, LANES), F32),
+                pltpu.VMEM((2 * n, rows, LANES), F32),
                 pltpu.VMEM((n, 1, chunk), F32),
                 pltpu.VMEM((rows, chunk), F32),
                 pltpu.VMEM((rows, chunk), F32),
                 pltpu.VMEM((2, quarter, LANES), F32),
-                pltpu.VMEM((2, quarter, LANES), F32),
-                pltpu.VMEM((n + 1, 2, quarter, LANES), F32),
-                pltpu.VMEM((quarter, chunk), BF16),
-                pltpu.VMEM((n, quarter, chunk), BF16),
+                pltpu.VMEM((2, rows, LANES), F32),
+                pltpu.VMEM((n, 2, quarter, LANES), F32),
+                pltpu.VMEM((quarter, n * LANES), BF16),
+                pltpu.VMEM((n, quarter, n * LANES), BF16),
                 pltpu.VMEM((3, max(n, nm), 8, 2 * rows), F32),
                 pltpu.VMEM((n, 1, chunk), F32),
                 pltpu.VMEM((1, chunk), F32),
                 pltpu.VMEM((1, width), F32),
-                dma((len(splits) + 2,)),
-                dma((24,)),
-                dma((24,)),
+                dma((len(splits) + 3,)),
+                dma((28,)),
+                dma((28,)),
             ],
             compiler_params=pltpu.CompilerParams(
                 collective_id=0, has_side_effects=True, vmem_limit_bytes=32 * 1024 * 1024
@@ -488,5 +586,5 @@
     in_specs = (P("dp", None, "mp"), P("dp", "mp"), P("dp"), P("mp"))
     out_specs = (P("dp", "mp"), P(None, "mp"), P("dp"), P("mp"))
     return jax.shard_map(
-        build(8, 8, (4, 4, 1)), mesh=mesh, in_specs=in_specs, out_specs=out_specs, check_vma=False
-    )
+        build(8, 8, (3, 3, 2)), mesh=mesh, in_specs=in_specs, out_specs=out_specs, check_vma=False
+    )

time: 68.5 us -> 64.3 us (0.939)
  the two profiles are of different devices: /device:TPU:1 before, /device:TPU:6 now
where the time goes in v4:
time: 64.3 us; the launch traced here: 63.6 us
  Pallas kernels  62.3 us (97%)
  between operations  1.29 us (2%)
    pallas_call x1, Pallas kernels, per_device(): pl.pallas_call(functools.partial(kernel, n, nm, splits), out_shape=(jax.S...  60.6 us
    pallas_call x1, Pallas kernels, per_device(): pl.pallas_call(writer, out_shape=tuple((jax.ShapeDtypeStruct(a.shape, a.d...  1.7 us

profile of v4, /device:TPU:6, one launch (start us, length us, event | category | flops | bytes accessed | tf_op | source)
XLA Modules:
  0.0 63.6 jit_solution(11812149085521981155)
XLA Ops:
  1.3 60.6 %shard_map.75 = (f32[1,9216]{1,0:T(1,128)S(1)}, bf16[64,9216]{1,0:T(8,128)(2,1)S(1)}, f32[1,1]{1,0:T(1,128)}, f32[1,9216]{1,0:T(1,128)S(1)}) custom-call(bf16[64,9216]{1,0:T(8,128)(2,1)} %bitcast.6, f32[1,9216]{1,0:T(1,128)} %master_ref.1, f32[1,1]{1,0:T(1,128)} %bitcast.5.row_state_ref, f32[1,9216]{1,0:T(1,128)} %bitcast.7), custom_call_target="tpu_custom_call" | custom-call | tf_op jit(solution)/shard_map/pallas_call | solution.py:535
  61.9 1.7 %shard_map.76 = (f32[1,9216]{1,0:T(1,128)}, bf16[64,9216]{1,0:T(8,128)(2,1)}, f32[1,1]{1,0:T(1,128)}, f32[1,9216]{1,0:T(1,128)}) custom-call(f32[1,9216]{1,0:T(1,128)S(1)} %get-tuple-element.12.refs_0_, bf16[64,9216]{1,0:T(8,128)(2,1)S(1)} %get-tuple-element.13.refs_1_, f32[1,1]{1,0:T(1,128)} %get-tuple-element.14.refs_2_, ...), custom_call_target="tpu_custom_call" | custom-call | tf_op jit(solution)/shard_map/pallas_call | solution.py:572

commit v5 on v4

--- a/solution.py
+++ b/solution.py
@@ -139,6 +139,11 @@
     here = cols(k * chunk, chunk)
     my_rows = pl.ds(pl.multiple_of(y * n, n), n)
 
+    barrier = pltpu.get_barrier_semaphore()
+    peers = [k_peer(d) for d in range(1, n)] + [y_peer(d) for d in range(1, n)] + [m_peer(d) for d in range(1, nm)]
+    for device in peers:
+        pl.semaphore_signal(barrier, inc=1, device_id=device, device_id_type=MESH)
+
     def extra_cols(yy):
         return tile(chunk_of_extra(yy) * per_chunk + n)
 
@@ -161,10 +166,6 @@
     own_state = pltpu.make_async_copy(col_state_ref, col_state, local_sem.at[len(splits) + 1])
     own_state.start()
 
-    barrier = pltpu.get_barrier_semaphore()
-    peers = [k_peer(d) for d in range(1, n)] + [y_peer(d) for d in range(1, n)] + [m_peer(d) for d in range(1, nm)]
-    for device in peers:
-        pl.semaphore_signal(barrier, inc=1, device_id=device, device_id_type=MESH)
     pl.semaphore_wait(barrier, len(peers))
 
     def part_group(first, count):
@@ -333,6 +334,16 @@
     def _():
         half_full[:, last] = half_x
 
+    for d in (1, 7):
+
+        @pl.when(y_of(d) < y_top)
+        def _():
+            half_copy(top, h_slot, d).start()
+
+        @pl.when(y_of(d) >= y_top)
+        def _():
+            half_copy(rows, hl_slot, d).start()
+
     col_chunk[:, mine] = col_new
     ccopy = start_all(
         col_chunk.at[:, seven_tiles],
@@ -377,7 +388,7 @@
 
     sums = collect(0, n, stat_group, sums)
     stat_group = exchange(1, nm, m_peer, sums)
-    for d in range(1, n):
+    for d in (4, 3, 5, 2, 6):
 
         @pl.when(y_of(d) < y_top)
         def _():
@@ -512,7 +523,12 @@
 def writer(*refs):
     *pairs, sem = refs
     count = len(pairs) // 2
-    copies = [pltpu.make_async_copy(pairs[i], pairs[count + i], sem.at[i]) for i in range(count)]
+    copies = []
+    for a, b in zip(pairs[:count], pairs[count:]):
+        step = min(a.shape[0], 16)
+        for r in range(0, a.shape[0], step):
+            piece = pl.ds(r, step)
+            copies.append(pltpu.make_async_copy(a.at[piece], b.at[piece], sem.at[len(copies)]))
     for c in copies:
         c.start()
     for c in copies:
@@ -562,8 +578,8 @@
                 pltpu.VMEM((1, chunk), F32),
                 pltpu.VMEM((1, width), F32),
                 dma((len(splits) + 3,)),
-                dma((28,)),
-                dma((28,)),
+                dma((26,)),
+                dma((26,)),
             ],
             compiler_params=pltpu.CompilerParams(
                 collective_id=0, has_side_effects=True, vmem_limit_bytes=32 * 1024 * 1024
@@ -574,7 +590,7 @@
             out_shape=tuple(jax.ShapeDtypeStruct(a.shape, a.dtype) for a in out),
             in_specs=[pl.BlockSpec(memory_space=pl.ANY)] * len(out),
             out_specs=tuple([hbm] * len(out)),
-            scratch_shapes=[dma((len(out),))],
+            scratch_shapes=[dma((len(out) - 1 + -(-rows // 16),))],
             compiler_params=pltpu.CompilerParams(vmem_limit_bytes=1024 * 1024),
         )(*out)
         return (master_new, weight_full, row_new.reshape(1), col_new.reshape(width))
@@ -586,5 +602,5 @@
     in_specs = (P("dp", None, "mp"), P("dp", "mp"), P("dp"), P("mp"))
     out_specs = (P("dp", "mp"), P(None, "mp"), P("dp"), P("mp"))
     return jax.shard_map(
-        build(8, 8, (3, 3, 2)), mesh=mesh, in_specs=in_specs, out_specs=out_specs, check_vma=False
+        build(8, 8, (4, 2, 1, 1)), mesh=mesh, in_specs=in_specs, out_specs=out_specs, check_vma=False
     )

time: 64.3 us -> 63.3 us (0.984)
    pallas_call x1, Pallas kernels: 60.6 us -> 59.9 us  [per_device(): pl.pallas_call(functools.partial(kernel, n, nm, splits), out_shape=(jax.S...]
where the time goes in v5:
time: 63.3 us; the launch traced here: 62.9 us
  Pallas kernels  61.7 us (97%)
  between operations  1.29 us (2%)
    pallas_call x1, Pallas kernels, per_device(): pl.pallas_call(functools.partial(kernel, n, nm, splits), out_shape=(jax.S...  59.9 us
    pallas_call x1, Pallas kernels, per_device(): pl.pallas_call(writer, out_shape=tuple((jax.ShapeDtypeStruct(a.shape, a.d...  1.72 us

profile of v5, /device:TPU:6, one launch (start us, length us, event | category | flops | bytes accessed | tf_op | source)
XLA Modules:
  0.0 62.9 jit_solution(14681013359146680141)
XLA Ops:
  1.3 59.9 %shard_map.75 = (f32[1,9216]{1,0:T(1,128)S(1)}, bf16[64,9216]{1,0:T(8,128)(2,1)S(1)}, f32[1,1]{1,0:T(1,128)}, f32[1,9216]{1,0:T(1,128)S(1)}) custom-call(bf16[64,9216]{1,0:T(8,128)(2,1)} %bitcast.6, f32[1,9216]{1,0:T(1,128)} %master_ref.1, f32[1,1]{1,0:T(1,128)} %bitcast.5.row_state_ref, f32[1,9216]{1,0:T(1,128)} %bitcast.7), custom_call_target="tpu_custom_call" | custom-call | tf_op jit(solution)/shard_map/pallas_call | solution.py:551
  61.2 1.7 %shard_map.76 = (f32[1,9216]{1,0:T(1,128)}, bf16[64,9216]{1,0:T(8,128)(2,1)}, f32[1,1]{1,0:T(1,128)}, f32[1,9216]{1,0:T(1,128)}) custom-call(f32[1,9216]{1,0:T(1,128)S(1)} %get-tuple-element.12.refs_0_, bf16[64,9216]{1,0:T(8,128)(2,1)S(1)} %get-tuple-element.13.refs_1_, f32[1,1]{1,0:T(1,128)} %get-tuple-element.14.refs_2_, ...), custom_call_target="tpu_custom_call" | custom-call | tf_op jit(solution)/shard_map/pallas_call | solution.py:588

commit v6 on v5

--- a/solution.py
+++ b/solution.py
@@ -334,7 +334,7 @@
     def _():
         half_full[:, last] = half_x
 
-    for d in (1, 7):
+    for d in (1, n - 1):
 
         @pl.when(y_of(d) < y_top)
         def _():
@@ -388,7 +388,7 @@
 
     sums = collect(0, n, stat_group, sums)
     stat_group = exchange(1, nm, m_peer, sums)
-    for d in (4, 3, 5, 2, 6):
+    for d in range(2, n - 1):
 
         @pl.when(y_of(d) < y_top)
         def _():
@@ -578,8 +578,8 @@
                 pltpu.VMEM((1, chunk), F32),
                 pltpu.VMEM((1, width), F32),
                 dma((len(splits) + 3,)),
-                dma((26,)),
-                dma((26,)),
+                dma((27,)),
+                dma((27,)),
             ],
             compiler_params=pltpu.CompilerParams(
                 collective_id=0, has_side_effects=True, vmem_limit_bytes=32 * 1024 * 1024
@@ -602,5 +602,5 @@
     in_specs = (P("dp", None, "mp"), P("dp", "mp"), P("dp"), P("mp"))
     out_specs = (P("dp", "mp"), P(None, "mp"), P("dp"), P("mp"))
     return jax.shard_map(
-        build(8, 8, (4, 2, 1, 1)), mesh=mesh, in_specs=in_specs, out_specs=out_specs, check_vma=False
+        build(8, 8, (3, 2, 1, 1, 1)), mesh=mesh, in_specs=in_specs, out_specs=out_specs, check_vma=False
     )

time: 63.3 us -> 63.5 us (level)
  no operation moved by 1% of the time
where the time goes in v6:
time: 63.5 us; the launch traced here: 63.4 us
  Pallas kernels  62.1 us (98%)
  between operations  1.29 us (2%)
    pallas_call x1, Pallas kernels, per_device(): pl.pallas_call(functools.partial(kernel, n, nm, splits), out_shape=(jax.S...  60.4 us
    pallas_call x1, Pallas kernels, per_device(): pl.pallas_call(writer, out_shape=tuple((jax.ShapeDtypeStruct(a.shape, a.d...  1.72 us

profile of v6, /device:TPU:6, one launch (start us, length us, event | category | flops | bytes accessed | tf_op | source)
XLA Modules:
  0.0 63.4 jit_solution(9722667406201135651)
XLA Ops:
  1.3 60.4 %shard_map.75 = (f32[1,9216]{1,0:T(1,128)S(1)}, bf16[64,9216]{1,0:T(8,128)(2,1)S(1)}, f32[1,1]{1,0:T(1,128)}, f32[1,9216]{1,0:T(1,128)S(1)}) custom-call(bf16[64,9216]{1,0:T(8,128)(2,1)} %bitcast.6, f32[1,9216]{1,0:T(1,128)} %master_ref.1, f32[1,1]{1,0:T(1,128)} %bitcast.5.row_state_ref, f32[1,9216]{1,0:T(1,128)} %bitcast.7), custom_call_target="tpu_custom_call" | custom-call | tf_op jit(solution)/shard_map/pallas_call | solution.py:551
  61.7 1.7 %shard_map.76 = (f32[1,9216]{1,0:T(1,128)}, bf16[64,9216]{1,0:T(8,128)(2,1)}, f32[1,1]{1,0:T(1,128)}, f32[1,9216]{1,0:T(1,128)}) custom-call(f32[1,9216]{1,0:T(1,128)S(1)} %get-tuple-element.12.refs_0_, bf16[64,9216]{1,0:T(8,128)(2,1)S(1)} %get-tuple-element.13.refs_1_, f32[1,1]{1,0:T(1,128)} %get-tuple-element.14.refs_2_, ...), custom_call_target="tpu_custom_call" | custom-call | tf_op jit(solution)/shard_map/pallas_call | solution.py:588
